TPU v7x, 32 devices: a whole 2x2x4 slice. The times are simulated.
32 devices in a mesh: item: 8 (over y, x, core), user: 4 (over z).
Axes of the slice: x: 2, y: 2, z: 4, core: 2. Of those that a mesh axis runs over, the one named last changes fastest.
Arguments:
- user_factors: bfloat16 [32256, 128], P(('user', 'item')), may hold values from -0.13 to 0.13
- ratings: bfloat16 [224, 32, 128], P('user', 'item'), may hold values from 0.049804688 to 5
- block_owner: int32 [8, 224], P('item', 'user'), may hold values from 0 to 3, as said below
- owner_block_position: int32 [8, 224], P('item', 'user'), may hold values from 0 to 62
- block_count: int32 [8, 4], P('item', 'user'), may hold values from 14 to 56, as said below
Outputs:
- item_factors: float32 [32, 128], P(('item', 'user'))
Inputs may be any that keep to these rules, and one draw needn't show every extreme that they name: `block_owner`: among the 56 blocks of one device no index of user is named more than 21 times; on every index of item one index of user is named exactly 21 times by the blocks of every index of user. `block_count`: on every index of item exactly one index of user holds 56 live blocks, the others 56 // 4 to 28; the live blocks are the first slots.
All inputs are finite; a program needn't handle non-finite values.
Results may differ from a plain program's by a relative error of at most 0.0003.
Values may be sent and summed in bfloat16 or wider, within the bound.
A program may use at most 64 MiB of HBM per device.

v0:
```python
import jax
import jax.numpy as jnp
from jax import lax
from jax.sharding import PartitionSpec as P

ITERS = 8


ridge_weight = 0.05
small_eps = 1e-06
group_blocks = 2


def conjugate_solve(system, right_side):
    solution = jnp.zeros_like(right_side)
    residual = right_side
    direction = right_side
    norm_now = jnp.sum(residual * residual, axis=-1, keepdims=True)
    for iteration in range(ITERS):
        image = jnp.einsum("jkl,jl->jk", system, direction, precision=lax.Precision.HIGHEST)
        alpha = norm_now / (jnp.sum(direction * image, axis=-1, keepdims=True) + small_eps)
        solution = solution + alpha * direction
        residual = residual - alpha * image
        norm_next = jnp.sum(residual * residual, axis=-1, keepdims=True)
        direction = residual + norm_next / (norm_now + small_eps) * direction
        norm_now = norm_next
    return solution


def block_terms(weights, block_rows, live_count, item_count):
    block_users = block_rows.shape[1]
    factor_width = block_rows.shape[2]
    group_turns = (live_count + group_blocks - 1) // group_blocks

    def accumulate(index_in_group, carry):
        gram_part, rhs_part = carry
        leading_slot = index_in_group * group_blocks
        w_group = lax.dynamic_slice_in_dim(weights, leading_slot, group_blocks, 0)
        r_group = lax.dynamic_slice_in_dim(block_rows, leading_slot, group_blocks, 0)
        live_mask = (leading_slot + jnp.arange(group_blocks, dtype=jnp.int32) < live_count).astype(
            jnp.bfloat16
        )
        w_group = w_group * live_mask[:, None, None]
        scaled = w_group[:, :, :, None] * r_group[:, None, :, :]
        gram_part = gram_part + jnp.einsum(
            "bjuk,bul->jkl", scaled, r_group, preferred_element_type=jnp.float32
        )
        live_ones = jnp.broadcast_to(live_mask[:, None], (group_blocks, block_users))
        rhs_part = rhs_part + jnp.einsum(
            "bju,buk->jk", w_group, r_group, preferred_element_type=jnp.float32
        )
        rhs_part = (
            rhs_part
            + jnp.einsum("bu,buk->k", live_ones, r_group, preferred_element_type=jnp.float32)[
                None, :
            ]
        )
        return (gram_part, rhs_part)

    initial = (
        jnp.zeros((item_count, factor_width, factor_width), jnp.float32),
        jnp.zeros((item_count, factor_width), jnp.float32),
    )
    gram_part, rhs_part = lax.fori_loop(0, group_turns, accumulate, initial)
    return jnp.concatenate([gram_part, rhs_part[:, None, :]], axis=1)


def on_device(user_factors, ratings, block_owner, owner_block_position, block_count):
    gathered = lax.all_gather(user_factors, "item", axis=0, tiled=True)
    block_users = ratings.shape[2]
    factor_width = gathered.shape[1]
    lookup = gathered.reshape(gathered.shape[0] // block_users, block_users, factor_width)
    owners = block_owner[0]
    local_ids = owner_block_position[0]
    filled = block_count[0, 0]
    peer_count = lax.axis_size("user")
    slot_count = owners.shape[0]
    capacity = max(2, 3 * slot_count // (2 * peer_count))
    onehot = (owners[:, None] == jnp.arange(peer_count, dtype=jnp.int32)[None, :]).astype(jnp.int32)
    before = jnp.cumsum(onehot, axis=0) - onehot
    position = jnp.sum(before * onehot, axis=1)
    requests = jnp.zeros((peer_count, capacity), jnp.int32).at[owners, position].set(local_ids)
    local_gram = jnp.einsum("rk,rl->kl", gathered, gathered, preferred_element_type=jnp.float32)
    fetched = lax.all_to_all(
        lookup[lax.all_to_all(requests, "user", split_axis=0, concat_axis=0, tiled=True)],
        "user",
        split_axis=0,
        concat_axis=0,
        tiled=True,
    )
    block_rows = fetched[owners, position]
    items_here = ratings.shape[1] // peer_count
    summed = lax.psum_scatter(
        block_terms(ratings, block_rows, filled, items_here * lax.axis_size("user")),
        "user",
        scatter_dimension=0,
        tiled=True,
    )
    system = summed[:, :factor_width, :]
    right_side = summed[:, factor_width, :]
    system = system + lax.psum(local_gram, "user")[None, :, :]
    system = system + ridge_weight * jnp.eye(factor_width, dtype=jnp.float32)[None, :, :]
    return conjugate_solve(system, right_side)


def solution(mesh):
    in_specs = (
        P(("user", "item"), None),
        P("user", "item", None),
        P("item", "user"),
        P("item", "user"),
        P("item", "user"),
    )
    out_specs = P(("item", "user"), None)
    return jax.shard_map(
        on_device, mesh=mesh, in_specs=in_specs, out_specs=out_specs, check_vma=False
    )
```

profile of v0, /device:TPU:0, one launch (start us, length us, event | category | flops | bytes accessed | tf_op | source)
XLA Modules:
  0.0 252.3 jit_solution(2925707396686532135)
XLA Ops:
  8.1 0.8 select_reduce_fusion
  9.6 5.7 %scatter_fusion = s32[4,21]{1,0:T(4,128)S(1)} fusion(s32[4,21]{1,0:T(4,128)S(1)} %broadcast.138, s32[56]{0:T(128)S(1)} %get-tuple-element.78, s32[56]{0:T(128)} %bitcast.166), kind=kCustom, calls=%fused_computation.2 | custom fusion | bytes 1120 | tf_op jit(solution)/shard_map/scatter | solution.py:82
  15.3 11.7 %all_to_all.17 = s32[4,1,21]{2,1,0:T(1,128)S(1)} all-to-all(s32[4,1,21]{2,1,0:T(1,128)S(1)} %bitcast.158), channel_id=1, replica_groups=mesh['item'=8,'user'=4] {'user'}, dimensions={0} | all-to-all | bytes 672 | tf_op jit(solution)/shard_map/all_to_all | solution.py:85
  27.1 12.6 %all-gather.2.cloned.1.call-done = bf16[8064,128]{1,0:T(8,128)(2,1)} async-done(((bf16[1008,128]{1,0:T(8,128)(2,1)}), bf16[8064,128]{1,0:T(8,128)(2,1)}) %all-gather.2.cloned.1.call-update) | async-done | bytes 2064400 | tf_op jit(solution)/shard_map/all_gather | solution.py:69
  39.7 4.2 %gather_fusion = bf16[84,128,128]{2,1,0:T(8,128)(2,1)} fusion(bf16[63,128,128]{2,1,0:T(8,128)(2,1)} %bitcast.159, s32[1024]{0:T(1024)S(1)} %pad_clamp_fusion), kind=kCustom, calls=%fused_computation | custom fusion | bytes 5505360 | tf_op jit(solution)/shard_map/gather | solution.py:85
  43.9 4.7 %all-to-all-start.1 = ((bf16[4,21,128,128]{3,2,1,0:T(8,128)(2,1)}), bf16[4,21,128,128]{3,2,1,0:T(8,128)(2,1)}, u32[]{:S(2)}, u32[]{:S(2)}) async-start(bf16[4,21,128,128]{3,2,1,0:T(8,128)(2,1)} %bitcast.160), calls=%async_computation.1 | async-start | bytes 5505024 | tf_op jit(solution)/shard_map/all_to_all | solution.py:84
  49.4 1.4 convolution_bitcast_fusion.3
  50.7 60.9 %all-to-all-done.1 = bf16[4,21,128,128]{3,2,1,0:T(8,128)(2,1)} async-done(((bf16[4,21,128,128]{3,2,1,0:T(8,128)(2,1)}), bf16[4,21,128,128]{3,2,1,0:T(8,128)(2,1)}, u32[]{:S(2)}, u32[]{:S(2)}) %all-to-all-start.1) | async-done | bytes 2752544 | tf_op jit(solution)/shard_map/all_to_all | solution.py:84
  111.7 2.8 %gather_fusion.1 = bf16[56,128,128]{2,1,0:T(8,128)(2,1)S(1)} fusion(bf16[4,21,128,128]{3,2,1,0:T(8,128)(2,1)} %all-to-all-done.1, s32[56]{0:T(128)S(1)} %bitcast.161), kind=kCustom, calls=%fused_computation.1 | custom fusion | bytes 3670464 | tf_op jit(solution)/shard_map/gather | solution.py:91
  114.5 26.1 %while.12 = (s32[]{:T(128)}, f32[4,128,128]{2,1,0:T(8,128)S(1)}, f32[4,128]{1,0:T(4,128)S(1)}, s32[]{:T(128)}, bf16[56,4,128]{2,1,0:T(4,128)(2,1)}, /*index=5*/s...) while((s32[]{:T(128)}, f32[4,128,128]{2,1,0:T(8,128)S(1)}, ...), condition=%wide.region_4.5_spmd, body=%wide.region_3.4_spmd.sunk | while | flops 34080780 | bytes 1066167 | solution.py:64
  115.2 0.8 dynamic-slice_multiply_fusion.2
  119.5 0.8 dynamic-slice_multiply_fusion.2
  130.4 0.8 dynamic-slice_multiply_fusion.2
  141.9 68.1 %all-reduce.4.cloned.1.call-done = (f32[4,129,128]{2,1,0:T(8,128)}, f32[1,128,128]{2,1,0:T(8,128)}) async-done(((f32[4,129,128]{2,1,0:T(8,128)}, f32[1,128,128]{2,1,0:T(8,128)}), (f32[4,129,128]{2,1,0:T(8,128)}, f32[1,128,128]{2,1,0:T(8,128)})) %all-reduce.4.cloned.1.call-update) | async-done | bytes 329744
  210.0 1.5 fusion.11
  211.6 1.9 multiply_reduce_fusion.13
  214.1 0.9 fusion.23
  218.3 0.9 multiply_reduce_fusion.11
  222.5 0.9 multiply_reduce_fusion.9
  226.7 0.9 multiply_reduce_fusion.7
  230.8 0.9 multiply_reduce_fusion.5
  235.0 0.9 multiply_reduce_fusion.3
  239.2 0.9 multiply_reduce_fusion.1
  242.7 0.9 fusion.9
  (126 shorter events, 31.7 us)
Async XLA Ops:
  6.5 33.2 %all-gather.2.cloned.1.call-start = ((), (), s32[]{:S(2)}) async-start(), calls=%async_computation.2 | async-start | bytes 2322432 | tf_op jit(solution)/shard_map/all_gather | solution.py:69
  43.9 5.4 %copy-start = (bf16[8064,128]{1,0:T(8,128)(2,1)S(1)}, bf16[8064,128]{1,0:T(8,128)(2,1)}, u32[]{:S(2)}) copy-start(bf16[8064,128]{1,0:T(8,128)(2,1)} %all-gather.2.cloned.1.call-done) | copy-start | bytes 6193156
  43.9 67.7 %all-to-all-start.1 = ((bf16[4,21,128,128]{3,2,1,0:T(8,128)(2,1)}), bf16[4,21,128,128]{3,2,1,0:T(8,128)(2,1)}, u32[]{:S(2)}, u32[]{:S(2)}) async-start(bf16[4,21,128,128]{3,2,1,0:T(8,128)(2,1)} %bitcast.160), calls=%async_computation.1 | async-start | bytes 5505024 | tf_op jit(solution)/shard_map/all_to_all | solution.py:84
  48.7 161.4 %all-reduce.4.cloned.1.call-start = ((), (), s32[]{:S(2)}) async-start(), calls=%async_computation.3 | async-start | bytes 688128
  114.5 26.8 %copy-start.1 = (u32[32]{0:T(128)S(1)}, u32[32]{0:T(128)}, u32[]{:S(2)}) copy-start(u32[32]{0:T(128)} %constant.99) | copy-start | bytes 388
Sparse Core Ops, SparseCore 0:
  9.2 30.4 all-gather.1
  141.5 68.5 all-reduce.3
where the time goes:
time: 254 us; the launch traced here: 252 us
  waiting for transfers between devices  142 us (56%)
  between operations  34.1 us (13%)
  other arithmetic  28.2 us (11%)
  matrix products  15.4 us (6%)
  local copies, waits for them, and re-layouts  15.2 us (6%)
  blocking collectives  11.7 us (5%)
  starting transfers between devices  4.75 us (2%)
    unnamed x3, waiting for transfers between devices  68.8 us
    all_to_all x1, waiting for transfers between devices, on_device(): lax.all_to_all(lookup[lax.all_to_all(requests, 'user', split_axis=0, conc...  60.9 us
    all_gather x1, waiting for transfers between devices, on_device(): gathered = lax.all_gather(user_factors, 'item', axis=0, tiled=True)  12.6 us
    all_to_all x1, blocking collectives, on_device(): lax.all_to_all(requests, 'user', split_axis=0, concat_axis=0, tiled=True)  11.7 us
    mul x12, other arithmetic, accumulate(): w_group = w_group * live_mask[:, None, None]  9.13 us
    convert_element_type x12, other arithmetic, accumulate(): (leading_slot + jnp.arange(group_blocks, dtype=jnp.int32) < live_count).a...  7.83 us
    dot_general x8, matrix products, conjugate_solve(): jnp.einsum('jkl,jl->jk', system, direction, precision=lax.Precision.HIGHEST)  7.2 us
    scatter x1, local copies, waits for them, and re-layouts, on_device(): jnp.zeros((peer_count, capacity), jnp.int32).at[owners, position]  5.75 us
  transfers between devices with their start and end apart: 3, of which 3 were waited for; matrix products, arithmetic and copies ran while one was open for 4% of the time, Pallas kernels for 0%

commit v1 on v0

--- a/solution.py
+++ b/solution.py
@@ -1,9 +1,12 @@
 import jax
 import jax.numpy as jnp
 from jax import lax
+from jax.experimental import pallas as pl
+from jax.experimental.pallas import tpu as pltpu
 from jax.sharding import PartitionSpec as P
 
 ITERS = 8
+MESH = pl.DeviceIdType.MESH
 
 
 ridge_weight = 0.05
@@ -103,6 +106,273 @@
     return conjugate_solve(system, right_side)
 
 
+def make_kernel(peer_count, item_count, rows_here, capacity, items_dev, weight_rows, factor_width, block_users):
+    chip_count = item_count // 2
+    half_chips = chip_count // 2
+    items_here = items_dev // peer_count
+    gram_rows = items_dev * factor_width
+    part_rows = factor_width + 8
+    tiles_here = rows_here // 16
+    block_tiles = block_users // 16
+
+    def kernel(
+        factors_ref, weights_ref, meta_ref, out_ref,
+        rows, weights_in, meta_in, places, acc, plain, part, part_in,
+        chip_send, chip_recv, twin_send, twin_recv,
+        weight_send, weight_recv, meta_send, meta_recv, part_send, part_recv, local_sem,
+    ):
+        me_item = lax.axis_index("item")
+        me_user = lax.axis_index("user")
+        core = lax.rem(me_item, 2)
+        chip = lax.div(me_item, 2)
+        chip_x = lax.rem(chip, 2)
+        chip_y = lax.div(chip, 2)
+        twin = chip * 2 + (1 - core)
+        shifts = [(dy, dx) for dy in range(half_chips) for dx in range(2) if dy or dx]
+
+        def chip_at(dy, dx):
+            return lax.rem(chip_y + dy, half_chips) * 2 + lax.rem(chip_x + dx, 2)
+
+        def shard(index):
+            return rows.at[pl.ds(index * tiles_here, tiles_here)]
+
+        barrier = pltpu.get_barrier_semaphore()
+        for dy, dx in shifts:
+            pl.semaphore_signal(
+                barrier, inc=1, device_id=(chip_at(dy, dx) * 2 + core, me_user), device_id_type=MESH
+            )
+        pl.semaphore_signal(barrier, inc=1, device_id=(twin, me_user), device_id_type=MESH)
+        for d in range(1, peer_count):
+            pl.semaphore_signal(
+                barrier, inc=1, device_id=(me_item, lax.rem(me_user + d, peer_count)), device_id_type=MESH
+            )
+        pl.semaphore_wait(barrier, len(shifts) + 1 + peer_count - 1)
+
+        def chip_copy(n, owner, target):
+            return pltpu.make_async_remote_copy(
+                src_ref=factors_ref, dst_ref=shard(owner),
+                send_sem=chip_send.at[n], recv_sem=chip_recv.at[n],
+                device_id=(target, me_user), device_id_type=MESH,
+            )
+
+        def twin_copy(n, src, owner):
+            return pltpu.make_async_remote_copy(
+                src_ref=src, dst_ref=shard(owner),
+                send_sem=twin_send.at[n], recv_sem=twin_recv.at[n],
+                device_id=(twin, me_user), device_id_type=MESH,
+            )
+
+        sent = []
+        for n, (dy, dx) in enumerate(shifts):
+            copy = chip_copy(n, me_item, chip_at(dy, dx) * 2 + core)
+            copy.start()
+            sent.append(copy)
+        copy = twin_copy(0, factors_ref, me_item)
+        copy.start()
+        sent.append(copy)
+        for d in range(1, peer_count):
+            target = lax.rem(me_user + d, peer_count)
+            copy = pltpu.make_async_remote_copy(
+                src_ref=meta_ref.at[target], dst_ref=meta_in.at[d],
+                send_sem=meta_send.at[d], recv_sem=meta_recv.at[d],
+                device_id=(me_item, target), device_id_type=MESH,
+            )
+            copy.start()
+            sent.append(copy)
+            copy = pltpu.make_async_remote_copy(
+                src_ref=weights_ref.at[target], dst_ref=weights_in.at[d],
+                send_sem=weight_send.at[d], recv_sem=weight_recv.at[d],
+                device_id=(me_item, target), device_id_type=MESH,
+            )
+            copy.start()
+            sent.append(copy)
+        own_weights = pltpu.make_async_copy(weights_ref.at[me_user], weights_in.at[0], local_sem.at[0])
+        own_meta = pltpu.make_async_copy(meta_ref.at[me_user], meta_in.at[0], local_sem.at[1])
+        own_rows = pltpu.make_async_copy(factors_ref, shard(me_item), local_sem.at[2])
+        own_weights.start()
+        own_meta.start()
+        own_rows.start()
+
+        def add_plain(block, first=False):
+            block = block.reshape(rows_here, factor_width)
+            term = lax.dot_general(
+                block, block, (((0,), (0,)), ((), ())), preferred_element_type=jnp.float32
+            )
+            plain[...] = term if first else plain[...] + term
+
+        add_plain(factors_ref[...], True)
+        acc[...] = jnp.zeros_like(acc)
+
+        def add_shard(index):
+            add_plain(rows[pl.ds(index * tiles_here, tiles_here)])
+
+        for n, (dy, dx) in enumerate(shifts):
+            owner = lax.rem(chip_y + half_chips - dy, half_chips) * 2 + lax.rem(chip_x + 2 - dx, 2)
+            owner = owner * 2 + core
+            chip_copy(n, owner, twin).wait_recv()
+            copy = twin_copy(n + 1, shard(owner), owner)
+            copy.start()
+            sent.append(copy)
+            add_shard(owner)
+        twin_copy(0, factors_ref, twin).wait_recv()
+        add_shard(twin)
+        for n, (dy, dx) in enumerate(shifts):
+            owner = lax.rem(chip_y + half_chips - dy, half_chips) * 2 + lax.rem(chip_x + 2 - dx, 2)
+            owner = owner * 2 + 1 - core
+            twin_copy(n + 1, shard(owner), owner).wait_recv()
+            add_shard(owner)
+        own_weights.wait()
+        own_meta.wait()
+        own_rows.wait()
+        for d in range(1, peer_count):
+            pltpu.make_async_remote_copy(
+                src_ref=meta_ref.at[0], dst_ref=meta_in.at[d],
+                send_sem=meta_send.at[d], recv_sem=meta_recv.at[d],
+                device_id=(twin, me_user), device_id_type=MESH,
+            ).wait_recv()
+            pltpu.make_async_remote_copy(
+                src_ref=weights_ref.at[0], dst_ref=weights_in.at[d],
+                send_sem=weight_send.at[d], recv_sem=weight_recv.at[d],
+                device_id=(twin, me_user), device_id_type=MESH,
+            ).wait_recv()
+        to_scalar = pltpu.make_async_copy(meta_in, places, local_sem.at[3])
+        to_scalar.start()
+        to_scalar.wait()
+
+        def slots(i, carry):
+            lefts, rights = [], []
+            for d in range(peer_count):
+                block = rows[pl.ds(places[d, 0, i] * block_tiles, block_tiles)]
+                block = block.reshape(block_users, factor_width)
+                turned = block.T
+                w = weights_in[d, i]
+                lefts.append(
+                    jnp.concatenate([turned * w[j : j + 1, :] for j in range(items_dev)] + [w], axis=0)
+                )
+                rights.append(block)
+            acc[...] += jnp.dot(
+                jnp.concatenate(lefts, axis=1),
+                jnp.concatenate(rights, axis=0),
+                preferred_element_type=jnp.float32,
+            )
+            return carry
+
+        lax.fori_loop(0, capacity, slots, 0)
+
+        common = plain[...]
+        live_sum = acc[gram_rows + items_dev : gram_rows + items_dev + 1, :]
+        for j in range(items_dev):
+            owner, place = j // items_here, j % items_here
+            part[owner, place, :factor_width, :] = (
+                acc[j * factor_width : (j + 1) * factor_width, :] + common
+            )
+            part[owner, place, factor_width:, :] = jnp.broadcast_to(
+                acc[gram_rows + j : gram_rows + j + 1, :] + live_sum, (8, factor_width)
+            )
+        for d in range(1, peer_count):
+            target = lax.rem(me_user + d, peer_count)
+            copy = pltpu.make_async_remote_copy(
+                src_ref=part.at[target], dst_ref=part_in.at[d - 1],
+                send_sem=part_send.at[d], recv_sem=part_recv.at[d],
+                device_id=(me_item, target), device_id_type=MESH,
+            )
+            copy.start()
+            sent.append(copy)
+        for d in range(1, peer_count):
+            pltpu.make_async_remote_copy(
+                src_ref=part.at[0], dst_ref=part_in.at[d - 1],
+                send_sem=part_send.at[d], recv_sem=part_recv.at[d],
+                device_id=(twin, me_user), device_id_type=MESH,
+            ).wait_recv()
+
+        row_at = lax.broadcasted_iota(jnp.int32, (factor_width, factor_width), 0)
+        col_at = lax.broadcasted_iota(jnp.int32, (factor_width, factor_width), 1)
+        diagonal = row_at == col_at
+        for place in range(items_here):
+            whole = part[me_user, place]
+            for d in range(1, peer_count):
+                whole = whole + part_in[d - 1, place]
+            system = whole[:factor_width] + jnp.where(diagonal, ridge_weight, 0.0)
+            residual = whole[factor_width : factor_width + 1]
+            answer = jnp.zeros_like(residual)
+            direction = residual
+            norm_now = jnp.sum(residual * residual, axis=1, keepdims=True)
+            for _ in range(ITERS):
+                image = jnp.sum(system * direction, axis=1, keepdims=True)
+                image = jnp.sum(jnp.where(diagonal, image, 0.0), axis=0, keepdims=True)
+                alpha = norm_now / (jnp.sum(direction * image, axis=1, keepdims=True) + small_eps)
+                answer = answer + alpha * direction
+                residual = residual - alpha * image
+                norm_next = jnp.sum(residual * residual, axis=1, keepdims=True)
+                direction = residual + norm_next / (norm_now + small_eps) * direction
+                norm_now = norm_next
+            out_ref[place : place + 1, :] = answer
+        for copy in sent:
+            copy.wait_send()
+
+    vmem = pl.BlockSpec(memory_space=pltpu.VMEM)
+    dma = pltpu.SemaphoreType.DMA
+    return pl.pallas_call(
+        kernel,
+        out_shape=jax.ShapeDtypeStruct((items_here, factor_width), jnp.float32),
+        in_specs=[vmem] * 3,
+        out_specs=vmem,
+        scratch_shapes=[
+            pltpu.VMEM((item_count * tiles_here, 16, factor_width), jnp.bfloat16),
+            pltpu.VMEM((peer_count, capacity, weight_rows, block_users), jnp.bfloat16),
+            pltpu.VMEM((peer_count, 8, 128), jnp.int32),
+            pltpu.SMEM((peer_count, 8, 128), jnp.int32),
+            pltpu.VMEM((gram_rows + weight_rows, factor_width), jnp.float32),
+            pltpu.VMEM((factor_width, factor_width), jnp.float32),
+            pltpu.VMEM((peer_count, items_here, part_rows, factor_width), jnp.float32),
+            pltpu.VMEM((peer_count - 1, items_here, part_rows, factor_width), jnp.float32),
+            dma((chip_count,)), dma((chip_count,)), dma((chip_count,)), dma((chip_count,)),
+            dma((peer_count,)), dma((peer_count,)), dma((peer_count,)), dma((peer_count,)),
+            dma((peer_count,)), dma((peer_count,)), dma((4,)),
+        ],
+        compiler_params=pltpu.CompilerParams(
+            collective_id=0, has_side_effects=True, vmem_limit_bytes=32 * 1024 * 1024
+        ),
+    )
+
+
+def sends_ratings(user_factors, ratings, block_owner, owner_block_position, block_count):
+    rows_here, factor_width = user_factors.shape
+    slot_count, items_dev, block_users = ratings.shape
+    peer_count = lax.axis_size("user")
+    item_count = lax.axis_size("item")
+    capacity = max(2, 3 * slot_count // (2 * peer_count))
+    weight_rows = (items_dev + 1 + 15) // 16 * 16
+    owners = block_owner[0]
+    local_ids = owner_block_position[0]
+    slot_at = jnp.arange(slot_count, dtype=jnp.int32)
+    earlier = (owners[None, :] == owners[:, None]) & (slot_at[None, :] < slot_at[:, None])
+    code = owners * capacity + jnp.sum(earlier.astype(jnp.int32), axis=1)
+    code = jnp.where(slot_at < block_count[0, 0], code, -1)
+    chosen = jnp.arange(peer_count * capacity, dtype=jnp.int32)[:, None] == code[None, :]
+    places = jnp.sum(jnp.where(chosen, local_ids[None, :], 0), axis=1).reshape(peer_count, 1, capacity)
+    meta = jnp.pad(places, ((0, 0), (0, 7), (0, 128 - capacity)))
+    padded = jnp.concatenate(
+        [
+            ratings,
+            jnp.ones((slot_count, 1, block_users), jnp.bfloat16),
+            jnp.zeros((slot_count, weight_rows - items_dev - 1, block_users), jnp.bfloat16),
+        ],
+        axis=1,
+    )
+    weights = jnp.einsum("rs,sju->rju", chosen.astype(jnp.bfloat16), padded)
+    weights = weights.reshape(peer_count, capacity, weight_rows, block_users)
+    kernel = make_kernel(
+        peer_count, item_count, rows_here, capacity, items_dev, weight_rows, factor_width, block_users
+    )
+    return kernel(user_factors.reshape(rows_here // 16, 16, factor_width), weights, meta)
+
+
+def by_shape(user_factors, ratings, block_owner, owner_block_position, block_count):
+    body = sends_ratings if user_factors.shape[0] % 16 == 0 else on_device
+    return body(user_factors, ratings, block_owner, owner_block_position, block_count)
+
+
 def solution(mesh):
     in_specs = (
         P(("user", "item"), None),
@@ -113,5 +383,5 @@
     )
     out_specs = P(("item", "user"), None)
     return jax.shard_map(
-        on_device, mesh=mesh, in_specs=in_specs, out_specs=out_specs, check_vma=False
-    )
+        by_shape, mesh=mesh, in_specs=in_specs, out_specs=out_specs, check_vma=False
+    )

time: 254 us -> 42.1 us (0.17)
  waiting for transfers between devices: 142 us -> 0 us
  Pallas kernels: 0 us -> 37.5 us
  between operations: 34.1 us -> 0.72 us
  other arithmetic: 28.2 us -> 0.28 us
  matrix products: 15.4 us -> 0.38 us
  local copies, waits for them, and re-layouts: 15.2 us -> 3 us
  blocking collectives: 11.7 us -> 0 us
  starting transfers between devices: 4.75 us -> 0 us
    unnamed x3 -> x0, waiting for transfers between devices: 68.8 us -> none
    all_to_all x1 -> x0, waiting for transfers between devices: 60.9 us -> none  [on_device(): lax.all_to_all(lookup[lax.all_to_all(requests, 'user', split_axis=0, conc...]
    pallas_call x0 -> x1, Pallas kernels: none -> 37.5 us  [sends_ratings(): kernel(user_factors.reshape(rows_here // 16, 16, factor_width), weights,...]
    dot_general x45 -> x1, matrix products: 15.4 us -> 0.38 us  [sends_ratings(): weights = jnp.einsum('rs,sju->rju', chosen.astype(jnp.bfloat16), padded)]
    all_gather x1 -> x0, waiting for transfers between devices: 12.6 us -> none  [on_device(): gathered = lax.all_gather(user_factors, 'item', axis=0, tiled=True)]
    all_to_all x1 -> x0, blocking collectives: 11.7 us -> none  [on_device(): lax.all_to_all(requests, 'user', split_axis=0, concat_axis=0, tiled=True)]
    mul x12 -> x0, other arithmetic: 9.13 us -> none  [accumulate(): w_group = w_group * live_mask[:, None, None]]
    convert_element_type x13 -> x0, other arithmetic: 8.55 us -> none  [the longest x12 7.83 us: accumulate(): (leading_slot + jnp.arange(group_blocks, dtype=jnp.int32) < live_count).a...]
  transfers between devices with their start and end apart: 3 -> 0, of which waited for: 3 -> 0; matrix products, arithmetic and copies ran while one was open for 4% -> 0% of each run, Pallas kernels for 0% -> 0%
where the time goes in v1:
time: 42.1 us; the launch traced here: 41.9 us
  Pallas kernels  37.5 us (89%)
  local copies, waits for them, and re-layouts  3 us (7%)
  between operations  0.72 us (2%)
    pallas_call x1, Pallas kernels, sends_ratings(): kernel(user_factors.reshape(rows_here // 16, 16, factor_width), weights,...  37.5 us
    unnamed x8, local copies, waits for them, and re-layouts  2.71 us

profile of v1, /device:TPU:0, one launch (start us, length us, event | category | flops | bytes accessed | tf_op | source)
XLA Modules:
  0.0 41.9 jit_solution(17021405131149206740)
XLA Ops:
  0.7 0.0 copy-start.1
  0.7 0.6 %copy-done.1 = s32[1,56]{1,0:T(1,128)S(1)} copy-done((s32[1,56]{1,0:T(1,128)S(1)}, s32[1,56]{1,0:T(1,128)}, u32[]{:S(2)}) %copy-start.1) | copy-done | bytes 248
  1.3 0.2 convert_reduce_fusion
  1.5 0.8 %copy.9 = bf16[56,4,128]{2,0,1:T(8,128)(2,1)S(1)} copy(bf16[56,4,128]{2,1,0:T(4,128)(2,1)} %param.6) | data formatting | bytes 114688 | tf_op args[1]
  2.3 0.1 pad.7.clone
  2.4 0.1 pad.6.clone
  2.5 0.4 fusion
  2.9 0.0 copy-start
  2.9 0.0 copy-start.2
  3.0 0.7 %copy-done.2 = s32[1,56]{1,0:T(1,128)S(1)} copy-done((s32[1,56]{1,0:T(1,128)S(1)}, s32[1,56]{1,0:T(1,128)}, u32[]{:S(2)}) %copy-start.2) | copy-done | bytes 248
  3.7 0.1 select_reduce_fusion
  3.8 0.1 reshape.20
  3.9 0.0 copy-done
  3.9 37.5 %shard_map.55 = f32[1,128]{1,0:T(1,128)S(1)} custom-call(bf16[63,16,128]{2,1,0:T(8,128)(2,1)S(1)} %bitcast.18, bf16[4,21,16,128]{3,2,1,0:T(8,128)(2,1)S(1)} %bitcast.17, s32[4,8,128]{2,1,0:T(8,128)S(1)} %pad.4.meta_ref), custom_call_target="tpu_custom_call" | custom-call | tf_op jit(solution)/shard_map/pallas_call | solution.py:368
  41.4 0.5 %copy.14 = f32[1,128]{1,0:T(1,128)} copy(f32[1,128]{1,0:T(1,128)S(1)} %shard_map.55) | data formatting | bytes 1024
  (4 shorter events, 0.1 us)
Async XLA Ops:
  0.7 0.7 %copy-start.1 = (s32[1,56]{1,0:T(1,128)S(1)}, s32[1,56]{1,0:T(1,128)}, u32[]{:S(2)}) copy-start(s32[1,56]{1,0:T(1,128)} %param.7) | copy-start | bytes 676
  2.9 1.0 %copy-start = (bf16[1008,128]{1,0:T(8,128)(2,1)S(1)}, bf16[1008,128]{1,0:T(8,128)(2,1)}, u32[]{:S(2)}) copy-start(bf16[1008,128]{1,0:T(8,128)(2,1)} %param.5) | copy-start | bytes 774148
  2.9 0.7 %copy-start.2 = (s32[1,56]{1,0:T(1,128)S(1)}, s32[1,56]{1,0:T(1,128)}, u32[]{:S(2)}) copy-start(s32[1,56]{1,0:T(1,128)} %param.8) | copy-start | bytes 676

commit v2 on v1

--- a/solution.py
+++ b/solution.py
@@ -133,8 +133,21 @@
         def chip_at(dy, dx):
             return lax.rem(chip_y + dy, half_chips) * 2 + lax.rem(chip_x + dx, 2)
 
+        across, along, corner = chip_at(0, 1), chip_at(1, 0), chip_at(1, 1)
+        first = tiles_here // 2
+        moves = [
+            (across, 0, across), (along, 1, along), (across, 1, across),
+            (along, 0, along), (corner, 0, along), (corner, 1, across),
+        ]
+
         def shard(index):
             return rows.at[pl.ds(index * tiles_here, tiles_here)]
+
+        def half_of(ref, start, half):
+            return ref.at[pl.ds(start + half * first, tiles_here - first if half else first)]
+
+        def half_shard(index, half):
+            return half_of(rows, index * tiles_here, half)
 
         barrier = pltpu.get_barrier_semaphore()
         for dy, dx in shifts:
@@ -148,26 +161,26 @@
             )
         pl.semaphore_wait(barrier, len(shifts) + 1 + peer_count - 1)
 
-        def chip_copy(n, owner, target):
+        def chip_copy(n, src, owner):
             return pltpu.make_async_remote_copy(
-                src_ref=factors_ref, dst_ref=shard(owner),
+                src_ref=src, dst_ref=half_shard(owner, moves[n][1]),
                 send_sem=chip_send.at[n], recv_sem=chip_recv.at[n],
-                device_id=(target, me_user), device_id_type=MESH,
-            )
-
-        def twin_copy(n, src, owner):
+                device_id=(moves[n][2] * 2 + core, me_user), device_id_type=MESH,
+            )
+
+        def twin_copy(n, src, dst):
             return pltpu.make_async_remote_copy(
-                src_ref=src, dst_ref=shard(owner),
+                src_ref=src, dst_ref=dst,
                 send_sem=twin_send.at[n], recv_sem=twin_recv.at[n],
                 device_id=(twin, me_user), device_id_type=MESH,
             )
 
         sent = []
-        for n, (dy, dx) in enumerate(shifts):
-            copy = chip_copy(n, me_item, chip_at(dy, dx) * 2 + core)
+        for n in range(4):
+            copy = chip_copy(n, half_of(factors_ref, 0, moves[n][1]), me_item)
             copy.start()
             sent.append(copy)
-        copy = twin_copy(0, factors_ref, me_item)
+        copy = twin_copy(6, factors_ref, shard(me_item))
         copy.start()
         sent.append(copy)
         for d in range(1, peer_count):
@@ -193,12 +206,12 @@
         own_meta.start()
         own_rows.start()
 
-        def add_plain(block, first=False):
+        def add_plain(block, opening=False):
             block = block.reshape(rows_here, factor_width)
             term = lax.dot_general(
                 block, block, (((0,), (0,)), ((), ())), preferred_element_type=jnp.float32
             )
-            plain[...] = term if first else plain[...] + term
+            plain[...] = term if opening else plain[...] + term
 
         add_plain(factors_ref[...], True)
         acc[...] = jnp.zeros_like(acc)
@@ -206,21 +219,39 @@
         def add_shard(index):
             add_plain(rows[pl.ds(index * tiles_here, tiles_here)])
 
-        for n, (dy, dx) in enumerate(shifts):
-            owner = lax.rem(chip_y + half_chips - dy, half_chips) * 2 + lax.rem(chip_x + 2 - dx, 2)
-            owner = owner * 2 + core
-            chip_copy(n, owner, twin).wait_recv()
-            copy = twin_copy(n + 1, shard(owner), owner)
-            copy.start()
-            sent.append(copy)
-            add_shard(owner)
-        twin_copy(0, factors_ref, twin).wait_recv()
+        def arrived(n):
+            piece = half_shard(moves[n][0] * 2 + core, moves[n][1])
+            chip_copy(n, piece, moves[n][0] * 2 + core).wait_recv()
+            if n < 2:
+                onward = chip_copy(n + 4, piece, moves[n][0] * 2 + core)
+                onward.start()
+                sent.append(onward)
+            handed = twin_copy(n, piece, piece)
+            handed.start()
+            sent.append(handed)
+
+        def twin_arrived(n):
+            piece = half_shard(moves[n][0] * 2 + 1 - core, moves[n][1])
+            twin_copy(n, piece, piece).wait_recv()
+
+        arrived(0)
+        arrived(1)
+        twin_copy(6, factors_ref, shard(twin)).wait_recv()
         add_shard(twin)
-        for n, (dy, dx) in enumerate(shifts):
-            owner = lax.rem(chip_y + half_chips - dy, half_chips) * 2 + lax.rem(chip_x + 2 - dx, 2)
-            owner = owner * 2 + 1 - core
-            twin_copy(n + 1, shard(owner), owner).wait_recv()
-            add_shard(owner)
+        arrived(2)
+        arrived(3)
+        add_shard(across * 2 + core)
+        add_shard(along * 2 + core)
+        for n in range(4):
+            twin_arrived(n)
+        add_shard(across * 2 + 1 - core)
+        add_shard(along * 2 + 1 - core)
+        arrived(4)
+        arrived(5)
+        add_shard(corner * 2 + core)
+        twin_arrived(4)
+        twin_arrived(5)
+        add_shard(corner * 2 + 1 - core)
         own_weights.wait()
         own_meta.wait()
         own_rows.wait()
@@ -257,7 +288,7 @@
             )
             return carry
 
-        lax.fori_loop(0, capacity, slots, 0)
+        lax.fori_loop(0, capacity, slots, 0, unroll=7)
 
         common = plain[...]
         live_sum = acc[gram_rows + items_dev : gram_rows + items_dev + 1, :]
@@ -326,7 +357,7 @@
             pltpu.VMEM((factor_width, factor_width), jnp.float32),
             pltpu.VMEM((peer_count, items_here, part_rows, factor_width), jnp.float32),
             pltpu.VMEM((peer_count - 1, items_here, part_rows, factor_width), jnp.float32),
-            dma((chip_count,)), dma((chip_count,)), dma((chip_count,)), dma((chip_count,)),
+            dma((6,)), dma((6,)), dma((7,)), dma((7,)),
             dma((peer_count,)), dma((peer_count,)), dma((peer_count,)), dma((peer_count,)),
             dma((peer_count,)), dma((peer_count,)), dma((4,)),
         ],
@@ -369,7 +400,8 @@
 
 
 def by_shape(user_factors, ratings, block_owner, owner_block_position, block_count):
-    body = sends_ratings if user_factors.shape[0] % 16 == 0 else on_device
+    fits = user_factors.shape[0] % 16 == 0 and lax.axis_size("item") == 8
+    body = sends_ratings if fits else on_device
     return body(user_factors, ratings, block_owner, owner_block_position, block_count)
 
 

time: 42.1 us -> 34.9 us (0.83)
  Pallas kernels: 37.5 us -> 30.3 us
    pallas_call x1, Pallas kernels: 37.5 us -> 30.3 us  [sends_ratings(): kernel(user_factors.reshape(rows_here // 16, 16, factor_width), weights,...]
where the time goes in v2:
time: 34.9 us; the launch traced here: 34.7 us
  Pallas kernels  30.3 us (87%)
  local copies, waits for them, and re-layouts  3 us (9%)
  between operations  0.72 us (2%)
  matrix products  0.38 us (1%)
    pallas_call x1, Pallas kernels, sends_ratings(): kernel(user_factors.reshape(rows_here // 16, 16, factor_width), weights,...  30.3 us
    unnamed x8, local copies, waits for them, and re-layouts  2.71 us

profile of v2, /device:TPU:0, one launch (start us, length us, event | category | flops | bytes accessed | tf_op | source)
XLA Modules:
  0.0 34.7 jit_solution(5976664883012278894)
XLA Ops:
  0.7 0.0 copy-start.1
  0.7 0.6 %copy-done.1 = s32[1,56]{1,0:T(1,128)S(1)} copy-done((s32[1,56]{1,0:T(1,128)S(1)}, s32[1,56]{1,0:T(1,128)}, u32[]{:S(2)}) %copy-start.1) | copy-done | bytes 248
  1.3 0.2 convert_reduce_fusion
  1.5 0.8 %copy.9 = bf16[56,4,128]{2,0,1:T(8,128)(2,1)S(1)} copy(bf16[56,4,128]{2,1,0:T(4,128)(2,1)} %param.6) | data formatting | bytes 114688 | tf_op args[1]
  2.3 0.1 pad.7.clone
  2.4 0.1 pad.6.clone
  2.5 0.4 %fusion = bf16[84,16,128]{2,0,1:T(8,128)(2,1)S(1)} fusion(bf16[56,4,128]{2,0,1:T(8,128)(2,1)S(1)} %copy.9, bf16[16]{0:T(256)(128)(2,1)S(1)} %pad.7.clone, bf16[16]{0:T(256)(128)(2,1)S(1)} %pad.6.clone, s32[56]{0:T(128)S(1)} %fusion.10), kind=kOutput, calls=%fused_computation | convolution fusion | flops 19960416 | bytes 401696 | tf_op jit(solution)/shard_map/rs,sju->rju/dot_general | solution.py:394
  2.9 0.0 copy-start
  2.9 0.0 copy-start.2
  3.0 0.7 %copy-done.2 = s32[1,56]{1,0:T(1,128)S(1)} copy-done((s32[1,56]{1,0:T(1,128)S(1)}, s32[1,56]{1,0:T(1,128)}, u32[]{:S(2)}) %copy-start.2) | copy-done | bytes 248
  3.7 0.1 select_reduce_fusion
  3.8 0.1 reshape.20
  3.9 0.0 copy-done
  3.9 30.3 %shard_map.55 = f32[1,128]{1,0:T(1,128)S(1)} custom-call(bf16[63,16,128]{2,1,0:T(8,128)(2,1)S(1)} %bitcast.18, bf16[4,21,16,128]{3,2,1,0:T(8,128)(2,1)S(1)} %bitcast.17, s32[4,8,128]{2,1,0:T(8,128)S(1)} %pad.4.meta_ref), custom_call_target="tpu_custom_call" | custom-call | tf_op jit(solution)/shard_map/pallas_call | solution.py:399
  34.2 0.5 %copy.14 = f32[1,128]{1,0:T(1,128)} copy(f32[1,128]{1,0:T(1,128)S(1)} %shard_map.55) | data formatting | bytes 1024
  (4 shorter events, 0.1 us)
Async XLA Ops:
  0.7 0.7 %copy-start.1 = (s32[1,56]{1,0:T(1,128)S(1)}, s32[1,56]{1,0:T(1,128)}, u32[]{:S(2)}) copy-start(s32[1,56]{1,0:T(1,128)} %param.7) | copy-start | bytes 676
  2.9 1.0 %copy-start = (bf16[1008,128]{1,0:T(8,128)(2,1)S(1)}, bf16[1008,128]{1,0:T(8,128)(2,1)}, u32[]{:S(2)}) copy-start(bf16[1008,128]{1,0:T(8,128)(2,1)} %param.5) | copy-start | bytes 774148
  2.9 0.7 %copy-start.2 = (s32[1,56]{1,0:T(1,128)S(1)}, s32[1,56]{1,0:T(1,128)}, u32[]{:S(2)}) copy-start(s32[1,56]{1,0:T(1,128)} %param.8) | copy-start | bytes 676

commit v3 on v2

--- a/solution.py
+++ b/solution.py
@@ -106,18 +106,21 @@
     return conjugate_solve(system, right_side)
 
 
-def make_kernel(peer_count, item_count, rows_here, capacity, items_dev, weight_rows, factor_width, block_users):
+def make_kernel(peer_count, item_count, rows_here, slot_count, capacity, items_dev, factor_width, block_users):
     chip_count = item_count // 2
     half_chips = chip_count // 2
     items_here = items_dev // peer_count
     gram_rows = items_dev * factor_width
     part_rows = factor_width + 8
+    weight_rows = (items_dev + 1 + 15) // 16 * 16
+    held = (capacity + 15) // 16 * 16
+    lanes = peer_count * held
     tiles_here = rows_here // 16
     block_tiles = block_users // 16
 
     def kernel(
-        factors_ref, weights_ref, meta_ref, out_ref,
-        rows, weights_in, meta_in, places, acc, plain, part, part_in,
+        factors_ref, ratings_ref, owners_ref, ids_ref, count_ref, out_ref,
+        rows, weights_out, weights_in, weights, meta_out, meta_in, places, acc, plain, part, part_in,
         chip_send, chip_recv, twin_send, twin_recv,
         weight_send, weight_recv, meta_send, meta_recv, part_send, part_recv, local_sem,
     ):
@@ -183,28 +186,53 @@
         copy = twin_copy(6, factors_ref, shard(me_item))
         copy.start()
         sent.append(copy)
-        for d in range(1, peer_count):
-            target = lax.rem(me_user + d, peer_count)
-            copy = pltpu.make_async_remote_copy(
-                src_ref=meta_ref.at[target], dst_ref=meta_in.at[d],
+        own_rows = pltpu.make_async_copy(factors_ref, shard(me_item), local_sem.at[0])
+        own_rows.start()
+
+        owners = jnp.broadcast_to(owners_ref[...], (slot_count, slot_count))
+        from_slot = lax.broadcasted_iota(jnp.int32, (slot_count, slot_count), 0)
+        to_slot = lax.broadcasted_iota(jnp.int32, (slot_count, slot_count), 1)
+        owners_down = jnp.sum(jnp.where(from_slot == to_slot, owners, 0), axis=1, keepdims=True)
+        earlier = (owners_down == owners) & (from_slot < to_slot)
+        rank = jnp.sum(jnp.where(earlier, 1, 0), axis=0, keepdims=True)
+        code = jnp.where(to_slot[:1] < count_ref[0, 0], owners[:1] * held + rank, -1)
+        chosen = lax.broadcasted_iota(jnp.int32, (lanes, slot_count), 0) == code
+        ids = jnp.broadcast_to(ids_ref[...], (lanes, slot_count))
+        ids_down = jnp.sum(jnp.where(chosen, ids, 0), axis=1, keepdims=True)
+        place_row = lax.broadcasted_iota(jnp.int32, (lanes, lanes), 0)
+        place_col = lax.broadcasted_iota(jnp.int32, (lanes, lanes), 1)
+        ids_across = jnp.sum(jnp.where(place_row == place_col, ids_down, 0), axis=0, keepdims=True)
+        meta_out[...] = jnp.broadcast_to(ids_across, (8, lanes))
+        meta_in[0] = meta_out[...]
+        picker = jnp.where(chosen, 1.0, 0.0).astype(jnp.bfloat16)
+        for j in range(items_dev + 1):
+            if j < items_dev:
+                plane = ratings_ref[:, j, :]
+            else:
+                plane = jnp.ones((slot_count, block_users), jnp.bfloat16)
+            picked = jnp.dot(picker, plane, preferred_element_type=jnp.float32).astype(jnp.bfloat16)
+            for d in range(peer_count):
+                weights_out[d, j] = picked[d * held : (d + 1) * held]
+
+        def meta_copy(d, target):
+            return pltpu.make_async_remote_copy(
+                src_ref=meta_out, dst_ref=meta_in.at[d],
                 send_sem=meta_send.at[d], recv_sem=meta_recv.at[d],
                 device_id=(me_item, target), device_id_type=MESH,
             )
-            copy.start()
-            sent.append(copy)
-            copy = pltpu.make_async_remote_copy(
-                src_ref=weights_ref.at[target], dst_ref=weights_in.at[d],
+
+        def weight_copy(d, target):
+            return pltpu.make_async_remote_copy(
+                src_ref=weights_out.at[target], dst_ref=weights_in.at[d - 1],
                 send_sem=weight_send.at[d], recv_sem=weight_recv.at[d],
                 device_id=(me_item, target), device_id_type=MESH,
             )
-            copy.start()
-            sent.append(copy)
-        own_weights = pltpu.make_async_copy(weights_ref.at[me_user], weights_in.at[0], local_sem.at[0])
-        own_meta = pltpu.make_async_copy(meta_ref.at[me_user], meta_in.at[0], local_sem.at[1])
-        own_rows = pltpu.make_async_copy(factors_ref, shard(me_item), local_sem.at[2])
-        own_weights.start()
-        own_meta.start()
-        own_rows.start()
+
+        for d in range(1, peer_count):
+            target = lax.rem(me_user + d, peer_count)
+            for copy in (meta_copy(d, target), weight_copy(d, target)):
+                copy.start()
+                sent.append(copy)
 
         def add_plain(block, opening=False):
             block = block.reshape(rows_here, factor_width)
@@ -242,44 +270,44 @@
         arrived(3)
         add_shard(across * 2 + core)
         add_shard(along * 2 + core)
+        for d in range(1, peer_count):
+            meta_copy(d, lax.rem(me_user + d, peer_count)).wait_recv()
+        to_scalar = pltpu.make_async_copy(meta_in, places, local_sem.at[1])
+        to_scalar.start()
+        weights[0] = weights_out[me_user].astype(jnp.float32)
+        for d in range(1, peer_count):
+            weight_copy(d, lax.rem(me_user + d, peer_count)).wait_recv()
+            weights[d] = weights_in[d - 1].astype(jnp.float32)
+        arrived(4)
+        arrived(5)
         for n in range(4):
             twin_arrived(n)
         add_shard(across * 2 + 1 - core)
         add_shard(along * 2 + 1 - core)
-        arrived(4)
-        arrived(5)
         add_shard(corner * 2 + core)
+        own_rows.wait()
+        to_scalar.wait()
         twin_arrived(4)
         twin_arrived(5)
         add_shard(corner * 2 + 1 - core)
-        own_weights.wait()
-        own_meta.wait()
-        own_rows.wait()
-        for d in range(1, peer_count):
-            pltpu.make_async_remote_copy(
-                src_ref=meta_ref.at[0], dst_ref=meta_in.at[d],
-                send_sem=meta_send.at[d], recv_sem=meta_recv.at[d],
-                device_id=(twin, me_user), device_id_type=MESH,
-            ).wait_recv()
-            pltpu.make_async_remote_copy(
-                src_ref=weights_ref.at[0], dst_ref=weights_in.at[d],
-                send_sem=weight_send.at[d], recv_sem=weight_recv.at[d],
-                device_id=(twin, me_user), device_id_type=MESH,
-            ).wait_recv()
-        to_scalar = pltpu.make_async_copy(meta_in, places, local_sem.at[3])
-        to_scalar.start()
-        to_scalar.wait()
+
+        extra_row = lax.broadcasted_iota(jnp.int32, (weight_rows, block_users), 0)
 
         def slots(i, carry):
             lefts, rights = [], []
             for d in range(peer_count):
-                block = rows[pl.ds(places[d, 0, i] * block_tiles, block_tiles)]
+                block = rows[pl.ds(places[d, 0, me_user * held + i] * block_tiles, block_tiles)]
                 block = block.reshape(block_users, factor_width)
                 turned = block.T
-                w = weights_in[d, i]
-                lefts.append(
-                    jnp.concatenate([turned * w[j : j + 1, :] for j in range(items_dev)] + [w], axis=0)
-                )
+                left = []
+                extra = jnp.zeros((weight_rows, block_users), jnp.float32)
+                for j in range(items_dev + 1):
+                    w = weights[d, j, pl.ds(i, 1), :]
+                    extra = jnp.where(extra_row == j, w, extra)
+                    if j < items_dev:
+                        left.append(turned * jnp.broadcast_to(w, turned.shape).astype(jnp.bfloat16))
+                left.append(extra.astype(jnp.bfloat16))
+                lefts.append(jnp.concatenate(left, axis=0))
                 rights.append(block)
             acc[...] += jnp.dot(
                 jnp.concatenate(lefts, axis=1),
@@ -346,20 +374,23 @@
     return pl.pallas_call(
         kernel,
         out_shape=jax.ShapeDtypeStruct((items_here, factor_width), jnp.float32),
-        in_specs=[vmem] * 3,
+        in_specs=[vmem] * 4 + [pl.BlockSpec(memory_space=pltpu.SMEM)],
         out_specs=vmem,
         scratch_shapes=[
             pltpu.VMEM((item_count * tiles_here, 16, factor_width), jnp.bfloat16),
-            pltpu.VMEM((peer_count, capacity, weight_rows, block_users), jnp.bfloat16),
-            pltpu.VMEM((peer_count, 8, 128), jnp.int32),
-            pltpu.SMEM((peer_count, 8, 128), jnp.int32),
+            pltpu.VMEM((peer_count, items_dev + 1, held, block_users), jnp.bfloat16),
+            pltpu.VMEM((peer_count - 1, items_dev + 1, held, block_users), jnp.bfloat16),
+            pltpu.VMEM((peer_count, items_dev + 1, held, block_users), jnp.float32),
+            pltpu.VMEM((8, lanes), jnp.int32),
+            pltpu.VMEM((peer_count, 8, lanes), jnp.int32),
+            pltpu.SMEM((peer_count, 8, lanes), jnp.int32),
             pltpu.VMEM((gram_rows + weight_rows, factor_width), jnp.float32),
             pltpu.VMEM((factor_width, factor_width), jnp.float32),
             pltpu.VMEM((peer_count, items_here, part_rows, factor_width), jnp.float32),
             pltpu.VMEM((peer_count - 1, items_here, part_rows, factor_width), jnp.float32),
             dma((6,)), dma((6,)), dma((7,)), dma((7,)),
             dma((peer_count,)), dma((peer_count,)), dma((peer_count,)), dma((peer_count,)),
-            dma((peer_count,)), dma((peer_count,)), dma((4,)),
+            dma((peer_count,)), dma((peer_count,)), dma((2,)),
         ],
         compiler_params=pltpu.CompilerParams(
             collective_id=0, has_side_effects=True, vmem_limit_bytes=32 * 1024 * 1024
@@ -373,30 +404,11 @@
     peer_count = lax.axis_size("user")
     item_count = lax.axis_size("item")
     capacity = max(2, 3 * slot_count // (2 * peer_count))
-    weight_rows = (items_dev + 1 + 15) // 16 * 16
-    owners = block_owner[0]
-    local_ids = owner_block_position[0]
-    slot_at = jnp.arange(slot_count, dtype=jnp.int32)
-    earlier = (owners[None, :] == owners[:, None]) & (slot_at[None, :] < slot_at[:, None])
-    code = owners * capacity + jnp.sum(earlier.astype(jnp.int32), axis=1)
-    code = jnp.where(slot_at < block_count[0, 0], code, -1)
-    chosen = jnp.arange(peer_count * capacity, dtype=jnp.int32)[:, None] == code[None, :]
-    places = jnp.sum(jnp.where(chosen, local_ids[None, :], 0), axis=1).reshape(peer_count, 1, capacity)
-    meta = jnp.pad(places, ((0, 0), (0, 7), (0, 128 - capacity)))
-    padded = jnp.concatenate(
-        [
-            ratings,
-            jnp.ones((slot_count, 1, block_users), jnp.bfloat16),
-            jnp.zeros((slot_count, weight_rows - items_dev - 1, block_users), jnp.bfloat16),
-        ],
-        axis=1,
-    )
-    weights = jnp.einsum("rs,sju->rju", chosen.astype(jnp.bfloat16), padded)
-    weights = weights.reshape(peer_count, capacity, weight_rows, block_users)
     kernel = make_kernel(
-        peer_count, item_count, rows_here, capacity, items_dev, weight_rows, factor_width, block_users
-    )
-    return kernel(user_factors.reshape(rows_here // 16, 16, factor_width), weights, meta)
+        peer_count, item_count, rows_here, slot_count, capacity, items_dev, factor_width, block_users
+    )
+    tiled = user_factors.reshape(rows_here // 16, 16, factor_width)
+    return kernel(tiled, ratings, block_owner, owner_block_position, block_count)
 
 
 def by_shape(user_factors, ratings, block_owner, owner_block_position, block_count):

time: 34.9 us -> 32.3 us (0.926)
  Pallas kernels: 30.3 us -> 28.4 us
  matrix products: 0.38 us -> 0 us
    pallas_call x1, Pallas kernels: 30.3 us -> 28.4 us  [sends_ratings(): kernel(tiled, ratings, block_owner, owner_block_position, block_count)]
    dot_general x1 -> x0, matrix products: 0.38 us -> none  [sends_ratings(): weights = jnp.einsum('rs,sju->rju', chosen.astype(jnp.bfloat16), padded)]
    unnamed x8 -> x9, local copies, waits for them, and re-layouts: 2.71 us -> 2.94 us
where the time goes in v3:
time: 32.3 us; the launch traced here: 32 us
  Pallas kernels  28.4 us (88%)
  local copies, waits for them, and re-layouts  2.94 us (9%)
  between operations  0.68 us (2%)
    pallas_call x1, Pallas kernels, sends_ratings(): kernel(tiled, ratings, block_owner, owner_block_position, block_count)  28.4 us
    unnamed x9, local copies, waits for them, and re-layouts  2.94 us

profile of v3, /device:TPU:0, one launch (start us, length us, event | category | flops | bytes accessed | tf_op | source)
XLA Modules:
  0.0 32.0 jit_solution(6224714824699428548)
XLA Ops:
  0.7 0.0 copy-start.2
  0.7 0.0 copy-start.3
  0.7 0.6 %copy-done.2 = s32[1,56]{1,0:T(1,128)S(1)} copy-done((s32[1,56]{1,0:T(1,128)S(1)}, s32[1,56]{1,0:T(1,128)}, u32[]{:S(2)}) %copy-start.2) | copy-done | bytes 248
  1.3 0.0 copy-done.3
  1.3 0.0 copy-start
  1.3 0.9 %copy-done = bf16[1008,128]{1,0:T(8,128)(2,1)S(1)} copy-done((bf16[1008,128]{1,0:T(8,128)(2,1)S(1)}, bf16[1008,128]{1,0:T(8,128)(2,1)}, u32[]{:S(2)}) %copy-start) | copy-done | bytes 258072
  2.3 0.0 copy-start.1
  2.3 0.8 %copy-done.1 = bf16[56,4,128]{2,1,0:T(4,128)(2,1)S(1)} copy-done((bf16[56,4,128]{2,1,0:T(4,128)(2,1)S(1)}, bf16[56,4,128]{2,1,0:T(4,128)(2,1)}, u32[]{:S(2)}) %copy-start.1) | copy-done | bytes 57368
  3.1 28.4 %shard_map.55 = f32[1,128]{1,0:T(1,128)S(1)} custom-call(bf16[63,16,128]{2,1,0:T(8,128)(2,1)S(1)} %bitcast.1, bf16[56,4,128]{2,1,0:T(4,128)(2,1)S(1)} %copy-done.1, s32[1,56]{1,0:T(1,128)S(1)} %copy-done.2, s32[1,56]{1,0:T(1,128)S(1)} %copy-done.3, s32[1,1]{1,0:T(1,128)S(6)} %copy.7.count_ref), custom_call_target="tpu_custom_call" | custom-call | tf_op jit(solution)/shard_map/pallas_call | solution.py:411
  31.5 0.5 %copy.8 = f32[1,128]{1,0:T(1,128)} copy(f32[1,128]{1,0:T(1,128)S(1)} %shard_map.55) | data formatting | bytes 1024
Async XLA Ops:
  0.7 0.7 %copy-start.2 = (s32[1,56]{1,0:T(1,128)S(1)}, s32[1,56]{1,0:T(1,128)}, u32[]{:S(2)}) copy-start(s32[1,56]{1,0:T(1,128)} %owners_ref.1) | copy-start | bytes 676
  0.7 0.7 %copy-start.3 = (s32[1,56]{1,0:T(1,128)S(1)}, s32[1,56]{1,0:T(1,128)}, u32[]{:S(2)}) copy-start(s32[1,56]{1,0:T(1,128)} %ids_ref.1) | copy-start | bytes 676
  1.3 0.9 %copy-start = (bf16[1008,128]{1,0:T(8,128)(2,1)S(1)}, bf16[1008,128]{1,0:T(8,128)(2,1)}, u32[]{:S(2)}) copy-start(bf16[1008,128]{1,0:T(8,128)(2,1)} %param.5) | copy-start | bytes 774148
  2.3 0.8 %copy-start.1 = (bf16[56,4,128]{2,1,0:T(4,128)(2,1)S(1)}, bf16[56,4,128]{2,1,0:T(4,128)(2,1)}, u32[]{:S(2)}) copy-start(bf16[56,4,128]{2,1,0:T(4,128)(2,1)} %ratings_ref.1) | copy-start | bytes 172036

commit v4 on v3

--- a/solution.py
+++ b/solution.py
@@ -110,7 +110,10 @@
     chip_count = item_count // 2
     half_chips = chip_count // 2
     items_here = items_dev // peer_count
-    gram_rows = items_dev * factor_width
+    order = [(d, place) for d in [*range(1, peer_count), 0] for place in range(items_here)]
+    first_items = items_dev // 2
+    gram_rows = first_items * factor_width
+    away = (peer_count - 1) * items_here
     part_rows = factor_width + 8
     weight_rows = (items_dev + 1 + 15) // 16 * 16
     held = (capacity + 15) // 16 * 16
@@ -119,8 +122,8 @@
     block_tiles = block_users // 16
 
     def kernel(
-        factors_ref, ratings_ref, owners_ref, ids_ref, count_ref, out_ref,
-        rows, weights_out, weights_in, weights, meta_out, meta_in, places, acc, plain, part, part_in,
+        factors_ref, ratings_ref, owners_far, ids_far, count_ref, out_ref,
+        rows, ratings_here, owners_ref, ids_ref, weights_out, weights_in, weights, meta_out, meta_in, places, acc, acc_last, plain, part, part_in,
         chip_send, chip_recv, twin_send, twin_recv,
         weight_send, weight_recv, meta_send, meta_recv, part_send, part_recv, local_sem,
     ):
@@ -152,6 +155,16 @@
         def half_shard(index, half):
             return half_of(rows, index * tiles_here, half)
 
+        own_rows = pltpu.make_async_copy(factors_ref, shard(me_item), local_sem.at[0])
+        own_rows.start()
+        own_ratings = pltpu.make_async_copy(ratings_ref, ratings_here, local_sem.at[2])
+        own_ratings.start()
+        own_slots = [
+            pltpu.make_async_copy(owners_far, owners_ref, local_sem.at[3]),
+            pltpu.make_async_copy(ids_far, ids_ref, local_sem.at[4]),
+        ]
+        for copy in own_slots:
+            copy.start()
         barrier = pltpu.get_barrier_semaphore()
         for dy, dx in shifts:
             pl.semaphore_signal(
@@ -186,9 +199,9 @@
         copy = twin_copy(6, factors_ref, shard(me_item))
         copy.start()
         sent.append(copy)
-        own_rows = pltpu.make_async_copy(factors_ref, shard(me_item), local_sem.at[0])
-        own_rows.start()
-
+
+        for copy in own_slots:
+            copy.wait()
         owners = jnp.broadcast_to(owners_ref[...], (slot_count, slot_count))
         from_slot = lax.broadcasted_iota(jnp.int32, (slot_count, slot_count), 0)
         to_slot = lax.broadcasted_iota(jnp.int32, (slot_count, slot_count), 1)
@@ -205,9 +218,10 @@
         meta_out[...] = jnp.broadcast_to(ids_across, (8, lanes))
         meta_in[0] = meta_out[...]
         picker = jnp.where(chosen, 1.0, 0.0).astype(jnp.bfloat16)
+        own_ratings.wait()
         for j in range(items_dev + 1):
             if j < items_dev:
-                plane = ratings_ref[:, j, :]
+                plane = ratings_here[:, j, :]
             else:
                 plane = jnp.ones((slot_count, block_users), jnp.bfloat16)
             picked = jnp.dot(picker, plane, preferred_element_type=jnp.float32).astype(jnp.bfloat16)
@@ -241,8 +255,10 @@
             )
             plain[...] = term if opening else plain[...] + term
 
-        add_plain(factors_ref[...], True)
+        own_rows.wait()
+        add_plain(rows[pl.ds(me_item * tiles_here, tiles_here)], True)
         acc[...] = jnp.zeros_like(acc)
+        acc_last[...] = jnp.zeros_like(acc_last)
 
         def add_shard(index):
             add_plain(rows[pl.ds(index * tiles_here, tiles_here)])
@@ -285,7 +301,6 @@
         add_shard(across * 2 + 1 - core)
         add_shard(along * 2 + 1 - core)
         add_shard(corner * 2 + core)
-        own_rows.wait()
         to_scalar.wait()
         twin_arrived(4)
         twin_arrived(5)
@@ -293,64 +308,74 @@
 
         extra_row = lax.broadcasted_iota(jnp.int32, (weight_rows, block_users), 0)
 
-        def slots(i, carry):
-            lefts, rights = [], []
-            for d in range(peer_count):
-                block = rows[pl.ds(places[d, 0, me_user * held + i] * block_tiles, block_tiles)]
-                block = block.reshape(block_users, factor_width)
-                turned = block.T
-                left = []
-                extra = jnp.zeros((weight_rows, block_users), jnp.float32)
-                for j in range(items_dev + 1):
-                    w = weights[d, j, pl.ds(i, 1), :]
-                    extra = jnp.where(extra_row == j, w, extra)
-                    if j < items_dev:
-                        left.append(turned * jnp.broadcast_to(w, turned.shape).astype(jnp.bfloat16))
-                left.append(extra.astype(jnp.bfloat16))
-                lefts.append(jnp.concatenate(left, axis=0))
-                rights.append(block)
-            acc[...] += jnp.dot(
-                jnp.concatenate(lefts, axis=1),
-                jnp.concatenate(rights, axis=0),
-                preferred_element_type=jnp.float32,
-            )
-            return carry
-
-        lax.fori_loop(0, capacity, slots, 0, unroll=7)
-
-        common = plain[...]
-        live_sum = acc[gram_rows + items_dev : gram_rows + items_dev + 1, :]
-        for j in range(items_dev):
-            owner, place = j // items_here, j % items_here
-            part[owner, place, :factor_width, :] = (
-                acc[j * factor_width : (j + 1) * factor_width, :] + common
-            )
-            part[owner, place, factor_width:, :] = jnp.broadcast_to(
-                acc[gram_rows + j : gram_rows + j + 1, :] + live_sum, (8, factor_width)
-            )
-        for d in range(1, peer_count):
-            target = lax.rem(me_user + d, peer_count)
-            copy = pltpu.make_async_remote_copy(
-                src_ref=part.at[target], dst_ref=part_in.at[d - 1],
-                send_sem=part_send.at[d], recv_sem=part_recv.at[d],
+        items = [lax.rem(me_user + d, peer_count) * items_here + place for d, place in order]
+
+        def add_slots(total, members, with_sides):
+            def slots(i, carry):
+                lefts, rights = [], []
+                for d in range(peer_count):
+                    block = rows[pl.ds(places[d, 0, me_user * held + i] * block_tiles, block_tiles)]
+                    block = block.reshape(block_users, factor_width)
+                    turned = block.T
+                    left = []
+                    extra = jnp.zeros((weight_rows, block_users), jnp.float32)
+                    for n, item in enumerate(items):
+                        if n in members or with_sides:
+                            w = weights[d, item, pl.ds(i, 1), :]
+                            extra = jnp.where(extra_row == n, w, extra)
+                        if n in members:
+                            left.append(turned * jnp.broadcast_to(w, turned.shape).astype(jnp.bfloat16))
+                    if with_sides:
+                        live = weights[d, items_dev, pl.ds(i, 1), :]
+                        extra = jnp.where(extra_row == items_dev, live, extra)
+                        left.append(extra.astype(jnp.bfloat16))
+                    lefts.append(jnp.concatenate(left, axis=0))
+                    rights.append(block)
+                total[...] += jnp.dot(
+                    jnp.concatenate(lefts, axis=1),
+                    jnp.concatenate(rights, axis=0),
+                    preferred_element_type=jnp.float32,
+                )
+                return carry
+
+            lax.fori_loop(0, capacity, slots, 0, unroll=7 if capacity % 7 == 0 else 1)
+
+        def part_copy(n):
+            target = lax.rem(me_user + order[n][0], peer_count)
+            return pltpu.make_async_remote_copy(
+                src_ref=part.at[n], dst_ref=part_in.at[n],
+                send_sem=part_send.at[n], recv_sem=part_recv.at[n],
                 device_id=(me_item, target), device_id_type=MESH,
             )
-            copy.start()
-            sent.append(copy)
-        for d in range(1, peer_count):
-            pltpu.make_async_remote_copy(
-                src_ref=part.at[0], dst_ref=part_in.at[d - 1],
-                send_sem=part_send.at[d], recv_sem=part_recv.at[d],
-                device_id=(twin, me_user), device_id_type=MESH,
-            ).wait_recv()
+
+        def finish(total, members):
+            live_sum = acc[gram_rows + items_dev : gram_rows + items_dev + 1, :]
+            for at, n in enumerate(members):
+                part[n, :factor_width, :] = (
+                    total[at * factor_width : (at + 1) * factor_width, :] + plain[...]
+                )
+                part[n, factor_width:, :] = jnp.broadcast_to(
+                    acc[gram_rows + n : gram_rows + n + 1, :] + live_sum, (8, factor_width)
+                )
+                if n < away:
+                    copy = part_copy(n)
+                    copy.start()
+                    sent.append(copy)
+
+        add_slots(acc, range(first_items), True)
+        finish(acc, range(first_items))
+        add_slots(acc_last, range(first_items, items_dev), False)
+        finish(acc_last, range(first_items, items_dev))
+        for n in range(away):
+            part_copy(n).wait_recv()
 
         row_at = lax.broadcasted_iota(jnp.int32, (factor_width, factor_width), 0)
         col_at = lax.broadcasted_iota(jnp.int32, (factor_width, factor_width), 1)
         diagonal = row_at == col_at
         for place in range(items_here):
-            whole = part[me_user, place]
+            whole = part[away + place]
             for d in range(1, peer_count):
-                whole = whole + part_in[d - 1, place]
+                whole = whole + part_in[(d - 1) * items_here + place]
             system = whole[:factor_width] + jnp.where(diagonal, ridge_weight, 0.0)
             residual = whole[factor_width : factor_width + 1]
             answer = jnp.zeros_like(residual)
@@ -370,14 +395,18 @@
             copy.wait_send()
 
     vmem = pl.BlockSpec(memory_space=pltpu.VMEM)
+    far = pl.BlockSpec(memory_space=pltpu.HBM)
     dma = pltpu.SemaphoreType.DMA
     return pl.pallas_call(
         kernel,
         out_shape=jax.ShapeDtypeStruct((items_here, factor_width), jnp.float32),
-        in_specs=[vmem] * 4 + [pl.BlockSpec(memory_space=pltpu.SMEM)],
+        in_specs=[far] * 4 + [pl.BlockSpec(memory_space=pltpu.SMEM)],
         out_specs=vmem,
         scratch_shapes=[
             pltpu.VMEM((item_count * tiles_here, 16, factor_width), jnp.bfloat16),
+            pltpu.VMEM((slot_count, items_dev, block_users), jnp.bfloat16),
+            pltpu.VMEM((1, slot_count), jnp.int32),
+            pltpu.VMEM((1, slot_count), jnp.int32),
             pltpu.VMEM((peer_count, items_dev + 1, held, block_users), jnp.bfloat16),
             pltpu.VMEM((peer_count - 1, items_dev + 1, held, block_users), jnp.bfloat16),
             pltpu.VMEM((peer_count, items_dev + 1, held, block_users), jnp.float32),
@@ -385,15 +414,16 @@
             pltpu.VMEM((peer_count, 8, lanes), jnp.int32),
             pltpu.SMEM((peer_count, 8, lanes), jnp.int32),
             pltpu.VMEM((gram_rows + weight_rows, factor_width), jnp.float32),
+            pltpu.VMEM(((items_dev - first_items) * factor_width, factor_width), jnp.float32),
             pltpu.VMEM((factor_width, factor_width), jnp.float32),
-            pltpu.VMEM((peer_count, items_here, part_rows, factor_width), jnp.float32),
-            pltpu.VMEM((peer_count - 1, items_here, part_rows, factor_width), jnp.float32),
+            pltpu.VMEM((items_dev, part_rows, factor_width), jnp.float32),
+            pltpu.VMEM((away, part_rows, factor_width), jnp.float32),
             dma((6,)), dma((6,)), dma((7,)), dma((7,)),
             dma((peer_count,)), dma((peer_count,)), dma((peer_count,)), dma((peer_count,)),
-            dma((peer_count,)), dma((peer_count,)), dma((2,)),
+            dma((away,)), dma((away,)), dma((5,)),
         ],
         compiler_params=pltpu.CompilerParams(
-            collective_id=0, has_side_effects=True, vmem_limit_bytes=32 * 1024 * 1024
+            collective_id=0, has_side_effects=True, vmem_limit_bytes=63 * 1024 * 1024
         ),
     )
 

time: 32.3 us -> 29.9 us (0.926)
  local copies, waits for them, and re-layouts: 2.94 us -> 1.19 us
  Pallas kernels: 28.4 us -> 27.9 us
    unnamed x9 -> x1, local copies, waits for them, and re-layouts: 2.94 us -> 1.19 us
    pallas_call x1, Pallas kernels: 28.4 us -> 27.9 us  [sends_ratings(): kernel(tiled, ratings, block_owner, owner_block_position, block_count)]
where the time goes in v4:
time: 29.9 us; the launch traced here: 29.8 us
  Pallas kernels  27.9 us (93%)
  local copies, waits for them, and re-layouts  1.19 us (4%)
  between operations  0.66 us (2%)
    pallas_call x1, Pallas kernels, sends_ratings(): kernel(tiled, ratings, block_owner, owner_block_position, block_count)  27.9 us
    unnamed x1, local copies, waits for them, and re-layouts  1.19 us

profile of v4, /device:TPU:0, one launch (start us, length us, event | category | flops | bytes accessed | tf_op | source)
XLA Modules:
  0.0 29.8 jit_solution(8407890617882292512)
XLA Ops:
  0.7 27.9 %shard_map.55 = f32[1,128]{1,0:T(1,128)} custom-call(bf16[63,16,128]{2,1,0:T(8,128)(2,1)} %bitcast.1, bf16[56,4,128]{2,1,0:T(4,128)(2,1)} %ratings_ref.1, s32[1,56]{1,0:T(1,128)} %owners_far.1, s32[1,56]{1,0:T(1,128)} %ids_far.1, s32[1,1]{1,0:T(1,128)S(6)} %copy.7.count_ref), custom_call_target="tpu_custom_call" | custom-call | tf_op jit(solution)/shard_map/pallas_call | solution.py:441
  28.6 1.2 %copy.8 = f32[1,128]{1,0:T(1,128)} copy(f32[1,128]{1,0:T(1,128)} %shard_map.55) | data formatting | bytes 1024

commit v5 on v4

--- a/solution.py
+++ b/solution.py
@@ -380,15 +380,25 @@
             residual = whole[factor_width : factor_width + 1]
             answer = jnp.zeros_like(residual)
             direction = residual
-            norm_now = jnp.sum(residual * residual, axis=1, keepdims=True)
+
+            def down(square):
+                return jnp.broadcast_to(jnp.sum(square, axis=1, keepdims=True), square.shape)
+
+            residual_down = down(jnp.where(diagonal, residual, 0.0))
+            direction_down = residual_down
+            norm_now = jnp.sum(residual_down * residual_down, axis=0, keepdims=True)
             for _ in range(ITERS):
-                image = jnp.sum(system * direction, axis=1, keepdims=True)
-                image = jnp.sum(jnp.where(diagonal, image, 0.0), axis=0, keepdims=True)
-                alpha = norm_now / (jnp.sum(direction * image, axis=1, keepdims=True) + small_eps)
+                image_down = down(system * direction)
+                image = jnp.sum(jnp.where(diagonal, image_down, 0.0), axis=0, keepdims=True)
+                curve = jnp.sum(direction_down * image_down, axis=0, keepdims=True)
+                alpha = norm_now / (curve + small_eps)
                 answer = answer + alpha * direction
                 residual = residual - alpha * image
-                norm_next = jnp.sum(residual * residual, axis=1, keepdims=True)
-                direction = residual + norm_next / (norm_now + small_eps) * direction
+                residual_down = residual_down - alpha * image_down
+                norm_next = jnp.sum(residual_down * residual_down, axis=0, keepdims=True)
+                beta = norm_next / (norm_now + small_eps)
+                direction = residual + beta * direction
+                direction_down = residual_down + beta * direction_down
                 norm_now = norm_next
             out_ref[place : place + 1, :] = answer
         for copy in sent:

time: 29.9 us -> 29 us (0.970)
  Pallas kernels: 27.9 us -> 27 us
    pallas_call x1, Pallas kernels: 27.9 us -> 27 us  [sends_ratings(): kernel(tiled, ratings, block_owner, owner_block_position, block_count)]
where the time goes in v5:
time: 29 us; the launch traced here: 28.8 us
  Pallas kernels  27 us (93%)
  local copies, waits for them, and re-layouts  1.19 us (4%)
  between operations  0.66 us (2%)
    pallas_call x1, Pallas kernels, sends_ratings(): kernel(tiled, ratings, block_owner, owner_block_position, block_count)  27 us
    unnamed x1, local copies, waits for them, and re-layouts  1.19 us

profile of v5, /device:TPU:0, one launch (start us, length us, event | category | flops | bytes accessed | tf_op | source)
XLA Modules:
  0.0 28.8 jit_solution(17132712821106807718)
XLA Ops:
  0.7 27.0 %shard_map.55 = f32[1,128]{1,0:T(1,128)} custom-call(bf16[63,16,128]{2,1,0:T(8,128)(2,1)} %bitcast.1, bf16[56,4,128]{2,1,0:T(4,128)(2,1)} %ratings_ref.1, s32[1,56]{1,0:T(1,128)} %owners_far.1, s32[1,56]{1,0:T(1,128)} %ids_far.1, s32[1,1]{1,0:T(1,128)S(6)} %copy.7.count_ref), custom_call_target="tpu_custom_call" | custom-call | tf_op jit(solution)/shard_map/pallas_call | solution.py:451
  27.6 1.2 %copy.8 = f32[1,128]{1,0:T(1,128)} copy(f32[1,128]{1,0:T(1,128)} %shard_map.55) | data formatting | bytes 1024
